TPU v7x, 256 devices: a whole 4x4x8 slice. The times are simulated.
256 devices in a mesh: gz: 8 (over x, core), yx: 32 (over y, z).
Axes of the slice: x: 4, y: 4, z: 8, core: 2. Of those that a mesh axis runs over, the one named last changes fastest.
Arguments:
- features: bfloat16 [16, 128, 512, 128], P(None, 'gz', 'yx'), may hold values from -19 to 19
- conv_weight: bfloat16 [3, 16, 3, 3, 3], replicated, may hold values from -0.3125 to 0.3125
- conv_bias: float32 [3], replicated, may hold values from -3 to 3
- labels: int32 [128, 512, 128], P('gz', 'yx'), may hold values from 0 to 8, as said below
Outputs:
- probabilities: float32 [8, 128, 512, 128], P(None, 'gz', 'yx')
- affinities: float32 [3, 128, 512, 128], P(None, 'gz', 'yx')
Inputs may be any that keep to these rules, and one draw needn't show every extreme that they name: `labels`: 0 marks an unseeded voxel, k marks a seed of colour k.
All inputs are finite; a program needn't handle non-finite values.
Results may differ from a plain program's by a relative error of at most 0.0012.
Values may be sent and summed in bfloat16 or wider, within the bound.
A program may use at most 64 MiB of HBM per device.

v0:
```python
import jax
import jax.numpy as jnp
from jax import lax
from jax.sharding import PartitionSpec as P

FIELDS = 8
ITERS = 3


RIDGE_WEIGHT = 0.5


def padded_2(cells, sides, width):
    for axis, dim in sides:
        count = lax.axis_size(axis)
        ends = count - 1
        head = lax.slice_in_dim(cells, 0, width, axis=dim)
        tail = lax.slice_in_dim(cells, cells.shape[dim] - width, cells.shape[dim], axis=dim)
        cells = jnp.concatenate(
            [
                lax.ppermute(tail, axis, [(i, (i + 1) % count) for i in range(ends)]),
                cells,
                lax.ppermute(head, axis, [((i + 1) % count, i) for i in range(ends)]),
            ],
            axis=dim,
        )
    return cells


def from_behind(value, axis, by):
    devices = lax.axis_size(axis)
    pairs = [(i, i + by) for i in range(devices) if 0 <= i + by < devices]
    return lax.ppermute(value, axis, pairs)


def conv_region(padded, conv_weight, count_z, count_y):
    col_cells = padded.shape[3] - 2
    summed = jnp.zeros((3, count_z, count_y, col_cells), jnp.float32)
    for offset_z in range(3):
        for offset_y in range(3):
            for offset_x in range(3):
                window = padded[
                    :,
                    offset_z : offset_z + count_z,
                    offset_y : offset_y + count_y,
                    offset_x : offset_x + col_cells,
                ]
                summed = summed + jnp.einsum(
                    "oc,czyx->ozyx",
                    conv_weight[:, :, offset_z, offset_y, offset_x],
                    window,
                    preferred_element_type=jnp.float32,
                )
    return summed


def stencil(field, padded, weights, seeded):
    weight_zup, weight_zdown, weight_yup, weight_ydown, weight_xup, weight_xdown = weights
    padded = jnp.pad(padded, ((0, 0), (0, 0), (0, 0), (1, 1)))
    laplace = weight_zup * (field - padded[:, 2:, 1:-1, 1:-1]) + weight_zdown * (
        field - padded[:, :-2, 1:-1, 1:-1]
    )
    laplace = (
        laplace
        + weight_yup * (field - padded[:, 1:-1, 2:, 1:-1])
        + weight_ydown * (field - padded[:, 1:-1, :-2, 1:-1])
    )
    laplace = (
        laplace
        + weight_xup * (field - padded[:, 1:-1, 1:-1, 2:])
        + weight_xdown * (field - padded[:, 1:-1, 1:-1, :-2])
    )
    return (1.0 - seeded) * (laplace + RIDGE_WEIGHT * field) + seeded * field


def operate(field, weights, seeded):
    padded = padded_2(field.astype(jnp.bfloat16), (("gz", 1), ("yx", 2)), 1).astype(field.dtype)
    return stencil(field, padded, weights, seeded)


def field_sums(left, right):
    return jnp.sum(left * right, axis=(1, 2, 3))


def spread_out(values):
    return values[:, None, None, None]


def squares(residual):
    return lax.psum(field_sums(residual, residual), ("gz", "yx"))


def body(features, conv_weight, conv_bias, labels):
    depth_cells = features.shape[1]
    row_cells = features.shape[2]
    col_cells = features.shape[3]
    global_z = lax.axis_index("gz") * depth_cells + jnp.arange(depth_cells, dtype=jnp.int32)
    global_y = lax.axis_index("yx") * row_cells + jnp.arange(row_cells, dtype=jnp.int32)
    keep_z = (global_z < depth_cells * lax.axis_size("gz") - 1).astype(jnp.float32)[:, None, None]
    keep_y = (global_y < row_cells * lax.axis_size("yx") - 1).astype(jnp.float32)[None, :, None]
    keep_x = (jnp.arange(col_cells, dtype=jnp.int32) < col_cells - 1).astype(jnp.float32)[
        None, None, :
    ]
    bias_column = conv_bias[:, None, None, None]
    padded = padded_2(features, (("gz", 1), ("yx", 2)), 1)
    padded = jnp.pad(padded, ((0, 0), (0, 0), (0, 0), (1, 1)))
    affinities = jax.nn.sigmoid(
        conv_region(padded, conv_weight, depth_cells, row_cells) + bias_column
    )
    below_plane = from_behind(affinities[0, -1], "gz", 1)
    below_row = from_behind(affinities[1, :, -1], "yx", 1)
    weight_zdown = jnp.concatenate([below_plane[None], affinities[0, :-1]], axis=0)
    weight_ydown = jnp.concatenate([below_row[:, None, :], affinities[1, :, :-1]], axis=1)
    weight_zup = affinities[0] * keep_z
    weight_yup = affinities[1] * keep_y
    weight_xup = affinities[2] * keep_x
    weight_xdown = jnp.pad(weight_xup, ((0, 0), (0, 0), (1, 0)))[:, :, :-1]
    weights = (
        weight_zup[None],
        weight_zdown[None],
        weight_yup[None],
        weight_ydown[None],
        weight_xup[None],
        weight_xdown[None],
    )
    seeded = (labels > 0).astype(jnp.float32)[None]
    colours = jnp.arange(1, FIELDS + 1, dtype=jnp.int32)[:, None, None, None]
    seed_field = (labels[None] == colours).astype(jnp.float32)
    right_side = seed_field - operate(seed_field, weights, seeded)
    solution = jnp.zeros_like(right_side)
    residual = right_side
    direction = right_side
    norm_now = squares(residual)
    for iteration in range(ITERS):
        applied = operate(direction, weights, seeded)
        curve = lax.psum(field_sums(direction, applied), ("gz", "yx"))
        step_size = norm_now / curve
        solution = solution + spread_out(step_size) * direction
        residual = residual - spread_out(step_size) * applied
        norm_next = squares(residual)
        direction = residual + spread_out(norm_next / norm_now) * direction
        norm_now = norm_next
    return (seed_field + solution, affinities)


def solution(mesh):
    in_specs = (P(None, "gz", "yx", None), P(), P(), P("gz", "yx", None))
    out_specs = (P(None, "gz", "yx", None), P(None, "gz", "yx", None))
    return jax.shard_map(body, mesh=mesh, in_specs=in_specs, out_specs=out_specs, check_vma=False)
```

profile of v0, /device:TPU:1, one launch (start us, length us, event | category | flops | bytes accessed | tf_op | source)
XLA Modules:
  0.0 506.8 jit_solution(4071813464939519983)
XLA Ops:
  0.7 3.0 copy.15
  4.5 4.5 collective-permute-start
  11.2 3.6 collective-permute-start.4
  20.2 3.5 collective-permute-start.6
  25.9 4.2 collective-permute-start.2
  47.4 4.1 collective-permute-start.8
  51.5 4.7 collective-permute-start.9
  63.1 3.3 collective-permute-done.11
  66.5 5.0 collective-permute-start.12
  73.0 5.0 collective-permute-done.13
  80.0 81.3 %all-reduce.6 = (f32[8]{0:T(128)S(1)}, f32[8]{0:T(128)S(1)}) all-reduce(f32[8]{0:T(128)S(1)} %get-tuple-element.7, f32[8]{0:T(128)S(1)} %get-tuple-element.6), channel_id=1, replica_groups=mesh['gz'=8,'yx'=32] {'gz','yx'}, use_global_device_ids=true, to_apply=%region_1.2 | all-reduce | flops 16 | bytes 128 | tf_op jit(solution)/shard_map/psum | solution.py:90
  162.1 73.2 %psum.44 = f32[8]{0:T(128)S(1)} all-reduce(f32[8]{0:T(128)S(1)} %get-tuple-element.16), channel_id=1, replica_groups=mesh['gz'=8,'yx'=32] {'gz','yx'}, use_global_device_ids=true, to_apply=%region_5.6 | all-reduce | flops 8 | bytes 64 | tf_op jit(solution)/shard_map/psum | solution.py:90
  236.3 3.3 collective-permute-start.14
  241.6 3.3 collective-permute-done.15
  245.0 3.7 collective-permute-start.16
  250.1 3.7 collective-permute-done.17
  256.6 75.5 %psum.45 = f32[8]{0:T(128)} all-reduce(f32[8]{0:T(128)S(1)} %get-tuple-element.12), channel_id=1, replica_groups=mesh['gz'=8,'yx'=32] {'gz','yx'}, use_global_device_ids=true, to_apply=%region_7.8 | all-reduce | flops 8 | bytes 64 | tf_op jit(solution)/shard_map/psum | solution.py:136
  334.2 72.6 %psum.46 = f32[8]{0:T(128)} all-reduce(f32[8]{0:T(128)S(1)} %multiply_reduce_fusion), channel_id=1, replica_groups=mesh['gz'=8,'yx'=32] {'gz','yx'}, use_global_device_ids=true, to_apply=%region_9.10 | all-reduce | flops 8 | bytes 64 | tf_op jit(solution)/shard_map/psum | solution.py:90
  409.1 3.0 collective-permute-start.18
  414.0 3.3 collective-permute-done.19
  417.4 3.7 collective-permute-start.20
  422.7 3.5 collective-permute-done.21
  428.2 76.0 %psum.47 = f32[8]{0:T(128)S(1)} all-reduce(f32[8]{0:T(128)S(1)} %fusion.133), channel_id=1, replica_groups=mesh['gz'=8,'yx'=32] {'gz','yx'}, use_global_device_ids=true, to_apply=%region_11.12 | all-reduce | flops 8 | bytes 64 | tf_op jit(solution)/shard_map/psum | solution.py:136
  504.2 2.5 convert_add_fusion
  (155 shorter events, 55.6 us)
Async XLA Ops:
  4.5 20.5 %collective-permute-start = (bf16[16,1,16,128]{3,0,2,1:T(8,128)(2,1)S(1)}, bf16[16,1,16,128]{3,0,2,1:T(8,128)(2,1)S(1)}, u32[]{:S(2)}, u32[]{:S(2)}) collective-permute-start(bf16[16,1,16,128]{3,0,2,1:T(8,128)(2,1)S(1)} %get-tuple-element.24), channel_id=1, source_target_pairs={{0,32},{32,64},{64,96},{96,128},{128,160},{160,192},{192,224},{1,3... | collective-permute-start | bytes 196616 | tf_op jit(solution)/shard_map/ppermute | solution.py:21
  9.0 16.8 %collective-permute-start.1 = (bf16[16,1,16,128]{3,0,2,1:T(8,128)(2,1)S(1)}, bf16[16,1,16,128]{3,0,2,1:T(8,128)(2,1)S(1)}, u32[]{:S(2)}, u32[]{:S(2)}) collective-permute-start(bf16[16,1,16,128]{3,0,2,1:T(8,128)(2,1)S(1)} %get-tuple-element.23), channel_id=1, source_target_pairs={{32,0},{64,32},{96,64},{128,96},{160,128},{192,160},{224,192},{33,... | collective-permute-start | bytes 196616 | tf_op jit(solution)/shard_map/ppermute | solution.py:23
  11.2 6.4 %collective-permute-start.4 = (bf16[8,1,16,128]{3,2,1,0:T(8,128)(2,1)S(1)}, bf16[8,1,16,128]{3,2,1,0:T(8,128)(2,1)S(1)}, u32[]{:S(2)}, u32[]{:S(2)}) collective-permute-start(bf16[8,1,16,128]{3,2,1,0:T(8,128)(2,1)S(1)} %get-tuple-element.43), channel_id=1, source_target_pairs={{0,32},{32,64},{64,96},{96,128},{128,160},{160,192},{192,224},{1,3... | collective-permute-start | bytes 98312 | tf_op jit(solution)/shard_map/ppermute | solution.py:21
  14.8 5.2 %collective-permute-start.5 = (bf16[8,1,16,128]{3,2,1,0:T(8,128)(2,1)S(1)}, bf16[8,1,16,128]{3,2,1,0:T(8,128)(2,1)S(1)}, u32[]{:S(2)}, u32[]{:S(2)}) collective-permute-start(bf16[8,1,16,128]{3,2,1,0:T(8,128)(2,1)S(1)} %get-tuple-element.44), channel_id=1, source_target_pairs={{32,0},{64,32},{96,64},{128,96},{160,128},{192,160},{224,192},{33,... | collective-permute-start | bytes 98312 | tf_op jit(solution)/shard_map/ppermute | solution.py:23
  20.2 14.3 %collective-permute-start.6 = (bf16[8,18,1,128]{3,2,1,0:T(2,128)(2,1)S(1)}, bf16[8,18,1,128]{3,2,1,0:T(2,128)(2,1)S(1)}, u32[]{:S(2)}, u32[]{:S(2)}) collective-permute-start(bf16[8,18,1,128]{3,2,1,0:T(2,128)(2,1)S(1)} %get-tuple-element.31), channel_id=1, source_target_pairs={{0,1},{1,2},{2,3},{3,4},{4,5},{5,6},{6,7},{7,8},{8,9},{9,10},{10,1... | collective-permute-start | bytes 110600 | tf_op jit(solution)/shard_map/ppermute | solution.py:21
  23.7 10.8 %collective-permute-start.7 = (bf16[8,18,1,128]{3,2,1,0:T(2,128)(2,1)S(1)}, bf16[8,18,1,128]{3,2,1,0:T(2,128)(2,1)S(1)}, u32[]{:S(2)}, u32[]{:S(2)}) collective-permute-start(bf16[8,18,1,128]{3,2,1,0:T(2,128)(2,1)S(1)} %get-tuple-element.32), channel_id=1, source_target_pairs={{1,0},{2,1},{3,2},{4,3},{5,4},{6,5},{7,6},{8,7},{9,8},{10,9},{11,1... | collective-permute-start | bytes 110600 | tf_op jit(solution)/shard_map/ppermute | solution.py:23
  25.9 9.1 %collective-permute-start.2 = (bf16[16,18,1,128]{3,0,2,1:T(8,128)(2,1)S(1)}, bf16[16,18,1,128]{3,0,2,1:T(8,128)(2,1)S(1)}, u32[]{:S(2)}, u32[]{:S(2)}) collective-permute-start(bf16[16,18,1,128]{3,0,2,1:T(8,128)(2,1)S(1)} %get-tuple-element.21), channel_id=1, source_target_pairs={{0,1},{1,2},{2,3},{3,4},{4,5},{5,6},{6,7},{7,8},{8,9},{9,10},{10,1... | collective-permute-start | bytes 221192 | tf_op jit(solution)/shard_map/ppermute | solution.py:21
  30.0 5.3 %collective-permute-start.3 = (bf16[16,18,1,128]{3,0,2,1:T(8,128)(2,1)S(1)}, bf16[16,18,1,128]{3,0,2,1:T(8,128)(2,1)S(1)}, u32[]{:S(2)}, u32[]{:S(2)}) collective-permute-start(bf16[16,18,1,128]{3,0,2,1:T(8,128)(2,1)S(1)} %get-tuple-element.22), channel_id=1, source_target_pairs={{1,0},{2,1},{3,2},{4,3},{5,4},{6,5},{7,6},{8,7},{9,8},{10,9},{11,1... | collective-permute-start | bytes 221192 | tf_op jit(solution)/shard_map/ppermute | solution.py:23
  47.4 9.8 %collective-permute-start.8 = (f32[16,128]{1,0:T(8,128)S(1)}, f32[16,128]{1,0:T(8,128)S(1)}, u32[]{:S(2)}, u32[]{:S(2)}) collective-permute-start(f32[16,128]{1,0:T(8,128)S(1)} %slice_bitcast_fusion), channel_id=1, source_target_pairs={{0,32},{32,64},{64,96},{96,128},{128,160},{160,192},{192,224},{1,3... | collective-permute-start | bytes 24584 | tf_op jit(solution)/shard_map/ppermute | solution.py:33
  51.5 5.6 %collective-permute-start.9 = (f32[16,128]{1,0:T(8,128)S(1)}, f32[16,128]{1,0:T(8,128)S(1)}, u32[]{:S(2)}, u32[]{:S(2)}) collective-permute-start(f32[16,128]{1,0:T(8,128)S(1)} %bitcast.231), channel_id=1, source_target_pairs={{0,1},{1,2},{2,3},{3,4},{4,5},{5,6},{6,7},{7,8},{8,9},{9,10},{10,1... | collective-permute-start | bytes 24584 | tf_op jit(solution)/shard_map/ppermute | solution.py:33
  58.6 4.5 collective-permute-start.10
  61.2 5.2 %collective-permute-start.11 = (bf16[8,1,16,128]{3,2,1,0:T(8,128)(2,1)S(1)}, bf16[8,1,16,128]{3,2,1,0:T(8,128)(2,1)S(1)}, u32[]{:S(2)}, u32[]{:S(2)}) collective-permute-start(bf16[8,1,16,128]{3,2,1,0:T(8,128)(2,1)S(1)} %get-tuple-element.38), channel_id=1, source_target_pairs={{32,0},{64,32},{96,64},{128,96},{160,128},{192,160},{224,192},{33,... | collective-permute-start | bytes 98312 | tf_op jit(solution)/shard_map/ppermute | solution.py:23
  66.5 6.4 %collective-permute-start.12 = (bf16[8,18,1,128]{3,2,1,0:T(2,128)(2,1)S(1)}, bf16[8,18,1,128]{3,2,1,0:T(2,128)(2,1)S(1)}, u32[]{:S(2)}, u32[]{:S(2)}) collective-permute-start(bf16[8,18,1,128]{3,2,1,0:T(2,128)(2,1)S(1)} %get-tuple-element.29), channel_id=1, source_target_pairs={{0,1},{1,2},{2,3},{3,4},{4,5},{5,6},{6,7},{7,8},{8,9},{9,10},{10,1... | collective-permute-start | bytes 110600 | tf_op jit(solution)/shard_map/ppermute | solution.py:21
  71.6 6.3 %collective-permute-start.13 = (bf16[8,18,1,128]{3,2,1,0:T(2,128)(2,1)S(1)}, bf16[8,18,1,128]{3,2,1,0:T(2,128)(2,1)S(1)}, u32[]{:S(2)}, u32[]{:S(2)}) collective-permute-start(bf16[8,18,1,128]{3,2,1,0:T(2,128)(2,1)S(1)} %get-tuple-element.30), channel_id=1, source_target_pairs={{1,0},{2,1},{3,2},{4,3},{5,4},{6,5},{7,6},{8,7},{9,8},{10,9},{11,1... | collective-permute-start | bytes 110600 | tf_op jit(solution)/shard_map/ppermute | solution.py:23
  235.3 96.8 %copy-start.23 = (f32[8]{0:T(128)}, f32[8]{0:T(128)S(1)}, u32[]{:S(2)}) copy-start(f32[8]{0:T(128)S(1)} %psum.44) | copy-start | bytes 100
  236.3 5.3 %collective-permute-start.14 = (bf16[8,1,16,128]{3,2,1,0:T(8,128)(2,1)S(1)}, bf16[8,1,16,128]{3,2,1,0:T(8,128)(2,1)S(1)}, u32[]{:S(2)}, u32[]{:S(2)}) collective-permute-start(bf16[8,1,16,128]{3,2,1,0:T(8,128)(2,1)S(1)} %get-tuple-element.35), channel_id=1, source_target_pairs={{0,32},{32,64},{64,96},{96,128},{128,160},{160,192},{192,224},{1,3... | collective-permute-start | bytes 98312 | tf_op jit(solution)/shard_map/ppermute | solution.py:21
  239.7 5.2 %collective-permute-start.15 = (bf16[8,1,16,128]{3,2,1,0:T(8,128)(2,1)S(1)}, bf16[8,1,16,128]{3,2,1,0:T(8,128)(2,1)S(1)}, u32[]{:S(2)}, u32[]{:S(2)}) collective-permute-start(bf16[8,1,16,128]{3,2,1,0:T(8,128)(2,1)S(1)} %get-tuple-element.36), channel_id=1, source_target_pairs={{32,0},{64,32},{96,64},{128,96},{160,128},{192,160},{224,192},{33,... | collective-permute-start | bytes 98312 | tf_op jit(solution)/shard_map/ppermute | solution.py:23
  245.0 5.1 %collective-permute-start.16 = (bf16[8,18,1,128]{3,2,1,0:T(2,128)(2,1)S(1)}, bf16[8,18,1,128]{3,2,1,0:T(2,128)(2,1)S(1)}, u32[]{:S(2)}, u32[]{:S(2)}) collective-permute-start(bf16[8,18,1,128]{3,2,1,0:T(2,128)(2,1)S(1)} %get-tuple-element.27), channel_id=1, source_target_pairs={{0,1},{1,2},{2,3},{3,4},{4,5},{5,6},{6,7},{7,8},{8,9},{9,10},{10,1... | collective-permute-start | bytes 110600 | tf_op jit(solution)/shard_map/ppermute | solution.py:21
  248.7 5.1 %collective-permute-start.17 = (bf16[8,18,1,128]{3,2,1,0:T(2,128)(2,1)S(1)}, bf16[8,18,1,128]{3,2,1,0:T(2,128)(2,1)S(1)}, u32[]{:S(2)}, u32[]{:S(2)}) collective-permute-start(bf16[8,18,1,128]{3,2,1,0:T(2,128)(2,1)S(1)} %get-tuple-element.28), channel_id=1, source_target_pairs={{1,0},{2,1},{3,2},{4,3},{5,4},{6,5},{7,6},{8,7},{9,8},{10,9},{11,1... | collective-permute-start | bytes 110600 | tf_op jit(solution)/shard_map/ppermute | solution.py:23
  409.1 4.9 collective-permute-start.18
  412.1 5.2 %collective-permute-start.19 = (bf16[8,1,16,128]{3,2,1,0:T(8,128)(2,1)S(1)}, bf16[8,1,16,128]{3,2,1,0:T(8,128)(2,1)S(1)}, u32[]{:S(2)}, u32[]{:S(2)}) collective-permute-start(bf16[8,1,16,128]{3,2,1,0:T(8,128)(2,1)S(1)} %get-tuple-element.34), channel_id=1, source_target_pairs={{32,0},{64,32},{96,64},{128,96},{160,128},{192,160},{224,192},{33,... | collective-permute-start | bytes 98312 | tf_op jit(solution)/shard_map/ppermute | solution.py:23
  417.4 5.3 %collective-permute-start.20 = (bf16[8,18,1,128]{3,2,1,0:T(2,128)(2,1)S(1)}, bf16[8,18,1,128]{3,2,1,0:T(2,128)(2,1)S(1)}, u32[]{:S(2)}, u32[]{:S(2)}) collective-permute-start(bf16[8,18,1,128]{3,2,1,0:T(2,128)(2,1)S(1)} %get-tuple-element.25), channel_id=1, source_target_pairs={{0,1},{1,2},{2,3},{3,4},{4,5},{5,6},{6,7},{7,8},{8,9},{9,10},{10,1... | collective-permute-start | bytes 110600 | tf_op jit(solution)/shard_map/ppermute | solution.py:21
  421.1 5.1 %collective-permute-start.21 = (bf16[8,18,1,128]{3,2,1,0:T(2,128)(2,1)S(1)}, bf16[8,18,1,128]{3,2,1,0:T(2,128)(2,1)S(1)}, u32[]{:S(2)}, u32[]{:S(2)}) collective-permute-start(bf16[8,18,1,128]{3,2,1,0:T(2,128)(2,1)S(1)} %get-tuple-element.26), channel_id=1, source_target_pairs={{1,0},{2,1},{3,2},{4,3},{5,4},{6,5},{7,6},{8,7},{9,8},{10,9},{11,1... | collective-permute-start | bytes 110600 | tf_op jit(solution)/shard_map/ppermute | solution.py:23
  426.7 77.5 %copy-start.22 = (f32[8]{0:T(128)S(1)}, f32[8]{0:T(128)}, u32[]{:S(2)}) copy-start(f32[8]{0:T(128)} %psum.46) | copy-start | bytes 100
  (23 other events, 434.5 us)
where the time goes:
time: 508 us; the launch traced here: 507 us
  blocking collectives  379 us (75%)
  starting transfers between devices  62.5 us (12%)
  waiting for transfers between devices  25.1 us (5%)
  other arithmetic  19.6 us (4%)
  matrix products  13.6 us (3%)
  local copies, waits for them, and re-layouts  5.78 us (1%)
    psum x3, blocking collectives, squares(): return lax.psum(field_sums(residual, residual), ('gz', 'yx'))  227 us
    psum x2, blocking collectives, body(): curve = lax.psum(field_sums(direction, applied), ('gz', 'yx'))  151 us
    ppermute x10, starting transfers between devices, padded_2(): lax.ppermute(tail, axis, [(i, (i + 1) % count) for i in range(ends)])  37.1 us
    ppermute x10, waiting for transfers between devices, padded_2(): lax.ppermute(head, axis, [((i + 1) % count, i) for i in range(ends)])  24.9 us
    ppermute x10, starting transfers between devices, padded_2(): lax.ppermute(head, axis, [((i + 1) % count, i) for i in range(ends)])  16.5 us
    dot_general x27, matrix products, conv_region(): jnp.einsum('oc,czyx->ozyx', conv_weight[:, :, offset_z, offset_y, offset_...  13.6 us
  transfers between devices with their start and end apart: 22, of which 10 were waited for; matrix products, arithmetic and copies ran while one was open for 1% of the time, Pallas kernels for 0%

commit v1 on v0

v1 whole, which is shorter than its diff:
```python
import jax
import jax.numpy as jnp
from jax import lax
from jax.experimental import pallas as pl
from jax.experimental.pallas import tpu as pltpu
from jax.sharding import PartitionSpec as P

MESH = pl.DeviceIdType.MESH
FIELDS = 8
ITERS = 3
RIDGE = 0.5
N = 16
X = 128
CH = 16
LOW = 3
EXT = N + 7
ROWS = 4 * (N + 2)
F32 = jnp.float32

STEP_LOW, STEP_HIGH = 1.0 / 12.5, 2.0
BETA_HIGH = 25.0


def lane_iota(shape):
    return lax.broadcasted_iota(jnp.int32, shape, len(shape) - 1)


def row_iota(shape):
    return lax.broadcasted_iota(jnp.int32, shape, len(shape) - 2)


def spread_row(row):
    return jnp.broadcast_to(row, (8, X))


def build_weights(taps_ref, lhs_ref):
    columns = 3 * CH * N
    expand = (lax.div(lane_iota((3 * CH, columns)), N) == row_iota((3 * CH, columns))).astype(jnp.bfloat16)
    taps = jnp.dot(taps_ref[...], expand, preferred_element_type=F32)
    y_in = lax.rem(lane_iota((8, columns)), N)
    half = lax.div(row_iota((8, columns)), 4)
    for dx in range(3):
        for pair in range(0, (N + 2) // 2, 2):
            blocks = []
            for p in (pair, pair + 1):
                if p >= (N + 2) // 2:
                    continue
                gap = y_in - (2 * p - 1 + half) + 1
                block = jnp.zeros((8, columns), F32)
                for dy in range(3):
                    at = (dy * 3 + dx) * 8
                    block = jnp.where(gap == dy, taps[at : at + 8], block)
                blocks.append(block)
            at = dx * 80 + pair * 8
            if len(blocks) == 1:
                blocks.append(jnp.zeros((8, columns), F32))
            lhs_ref[at : at + 16, :] = jnp.concatenate(blocks, axis=0).astype(jnp.bfloat16)


def sigmoid(x):
    e = jnp.exp(-jnp.abs(x))
    s = 1.0 / (1.0 + e)
    return jnp.where(x >= 0.0, s, e * s)


def kernel(
    feat_ref, taps_ref, bias_ref, labels_ref,
    prob_ref, aff_ref,
    feat, lhs, lab, own, row19,
    y_low, y_high, z_low, z_high, low_low, low_high, high_low, high_high, row19_in,
    raw, edge, seed, w0, w1, w2,
    part, sum_z, sum_y,
    feat_sem, send_sem, recv_sem, psend_sem, precv_sem,
):
    gz, yx = lax.axis_index("gz"), lax.axis_index("yx")
    nz, ny = lax.axis_size("gz"), lax.axis_size("yx")
    z_up, z_dn = lax.rem(gz + 1, nz), lax.rem(gz + nz - 1, nz)
    y_up, y_dn = lax.rem(yx + 1, ny), lax.rem(yx + ny - 1, ny)

    loads = [
        pltpu.make_async_copy(feat_ref.at[c], feat.at[pl.ds(2, N), pl.ds(c * N, N), :], feat_sem.at[c])
        for c in range(CH)
    ]
    for load in loads:
        load.start()

    barrier = pltpu.get_barrier_semaphore()
    count = 0
    for dz in (z_dn, gz, z_up):
        for dy in (y_dn, yx, y_up):
            if dz is gz and dy is yx:
                continue
            pl.semaphore_signal(barrier, inc=1, device_id=(dz, dy), device_id_type=MESH)
            count += 1
    for i in range(2, nz - 1):
        pl.semaphore_signal(barrier, inc=1, device_id=(lax.rem(gz + i, nz), yx), device_id_type=MESH)
        count += 1
    for i in range(2, ny - 1):
        pl.semaphore_signal(barrier, inc=1, device_id=(gz, lax.rem(yx + i, ny)), device_id_type=MESH)
        count += 1

    for p in (0, 1, N + 2, N + 3):
        feat[p] = jnp.zeros((CH * N, X), jnp.bfloat16)
    lab[0] = jnp.zeros((N, X), F32)
    lab[N + 1] = jnp.zeros((N, X), F32)
    for z in range(N):
        lab[z + 1] = labels_ref[z].astype(F32)
    for z in range(N):
        row19[z : z + 1, :] = lab[z + 1, 3:4, :]
    build_weights(taps_ref, lhs)

    for load in loads:
        load.wait()

    sublane = row_iota((8, X))
    lane = lane_iota((8, X))
    first, last = lane == 0, lane == X - 1

    def two_planes(j, carry):
        plane = 2 * j
        left = feat[pl.ds(plane, 3)].reshape(3 * CH * N, X)
        right = feat[pl.ds(plane + 1, 3)].reshape(3 * CH * N, X)
        both = jnp.concatenate([left, right], axis=1)
        out = jnp.dot(lhs[...], both, preferred_element_type=F32)
        for h in range(2):
            for p in range((N + 2) // 2):
                at = 8 * p
                a = out[at : at + 8, h * X : (h + 1) * X]
                b = out[80 + at : 80 + at + 8, h * X : (h + 1) * X]
                c = out[160 + at : 160 + at + 8, h * X : (h + 1) * X]
                total = (
                    b
                    + jnp.where(first, 0.0, pltpu.roll(a, 1, 1))
                    + jnp.where(last, 0.0, pltpu.roll(c, X - 1, 1))
                )
                y = 2 * p - 1
                if y >= 0:
                    total = jnp.where(sublane == 3, spread_row(lab[plane + h, y : y + 1, :]), total)
                if y + 1 < N:
                    total = jnp.where(sublane == 7, spread_row(lab[plane + h, y + 1 : y + 2, :]), total)
                own[plane + h, at : at + 8, :] = total
        return carry

    lax.fori_loop(0, (N + 2) // 2, two_planes, 0)

    pl.semaphore_wait(barrier, count)

    bottom, top = pl.ds(0, 16), pl.ds(ROWS - 16, 16)
    sends = [
        (own.at[:, top, :], y_low, (gz, y_up)),
        (own.at[:, bottom, :], y_high, (gz, y_dn)),
        (own.at[pl.ds(N - 2, 4)], z_low, (z_up, yx)),
        (own.at[pl.ds(0, 5)], z_high, (z_dn, yx)),
        (own.at[pl.ds(N - 2, 4), top, :], low_low, (z_up, y_up)),
        (own.at[pl.ds(N - 2, 4), bottom, :], low_high, (z_up, y_dn)),
        (own.at[pl.ds(0, 4), top, :], high_low, (z_dn, y_up)),
        (own.at[pl.ds(0, 4), bottom, :], high_high, (z_dn, y_dn)),
        (row19, row19_in, (gz, y_dn)),
    ]
    copies = []
    for i, (src, dst, to) in enumerate(sends):
        copy = pltpu.make_async_remote_copy(
            src_ref=src, dst_ref=dst, send_sem=send_sem.at[i], recv_sem=recv_sem.at[i], device_id=to, device_id_type=MESH
        )
        copy.start()
        copies.append(copy)
    for copy in copies:
        copy.wait()

    has_zl, has_zh = (gz > 0).astype(F32), (gz < nz - 1).astype(F32)
    has_yl, has_yh = (yx > 0).astype(F32), (yx < ny - 1).astype(F32)
    kind = lax.rem(sublane, 4)
    bias = jnp.where(kind == 0, bias_ref[0], jnp.where(kind == 1, bias_ref[1], bias_ref[2]))
    keep_x = jnp.where((kind == 2) & last, 0.0, 1.0)
    is_label = kind == 3

    def plane_weights(plane, own_plane, zn, zn_plane, has_z, corner_low, corner_high, yn_plane):
        z = plane - LOW
        global_z = gz * N + z
        inside = jnp.logical_and(global_z >= 0, global_z < nz * N - 1).astype(F32)
        keep_zx = jnp.where(kind == 0, inside, keep_x)
        for v in range(11):
            terms = []
            if 1 <= v <= 9:
                if own_plane is not None:
                    terms.append(own[own_plane, 8 * (v - 1) : 8 * v, :])
                if zn is not None:
                    terms.append(has_z * zn[zn_plane, 8 * (v - 1) : 8 * v, :])
            if v <= 1:
                if yn_plane is not None:
                    terms.append(has_yl * y_low[yn_plane, 8 * v : 8 * v + 8, :])
                if corner_low is not None:
                    terms.append((has_yl * has_z) * corner_low[zn_plane, 8 * v : 8 * v + 8, :])
            if v >= 9:
                if yn_plane is not None:
                    terms.append(has_yh * y_high[yn_plane, 8 * (v - 9) : 8 * (v - 9) + 8, :])
                if corner_high is not None:
                    terms.append((has_yh * has_z) * corner_high[zn_plane, 8 * (v - 9) : 8 * (v - 9) + 8, :])
            total = terms[0]
            for term in terms[1:]:
                total = total + term
            a = jnp.where(is_label, total, sigmoid(total + bias))
            raw[plane, 8 * v : 8 * v + 8, :] = a
            keep = keep_zx
            if v == 1:
                keep = jnp.where(sublane == 1, has_yl, keep)
            if v == 9:
                keep = jnp.where(sublane == 1, has_yh, keep)
            edge[plane, 8 * v : 8 * v + 8, :] = jnp.where(is_label, (a == 0.0).astype(F32), a * keep)

    for z in (-3, -2):
        plane_weights(z + LOW, None, z_low, z + 3, has_zl, low_low, low_high, None)
    for z in (-1, 0):
        plane_weights(z + LOW, z + 1, z_low, z + 3, has_zl, low_low, low_high, z + 1)

    def middle(z, carry):
        plane_weights(z + LOW, z + 1, None, None, None, None, None, z + 1)
        return carry

    lax.fori_loop(1, N - 1, middle, 0)
    for z in (15, 16):
        plane_weights(z + LOW, z + 1, z_high, z - 15, has_zh, high_low, high_high, z + 1)
    for z in (17, 18):
        plane_weights(z + LOW, None, z_high, z - 15, has_zh, high_low, high_high, None)

    def affinities_out(z, carry):
        for o in range(3):
            for h in range(2):
                at = pl.multiple_of(o * N * N + z * N + 8 * h, 8)
                aff_ref[pl.ds(at, 8), :] = raw[z + LOW, pl.ds(4 * LOW + 32 * h + o, 8, stride=4), :]
        return carry

    lax.fori_loop(0, N, affinities_out, 0)

    colour = (sublane + 1).astype(F32)

    def seeds(plane, carry):
        for y in range(EXT - 1):
            label = spread_row(raw[plane, 4 * y + 3 : 4 * y + 4, :])
            seed[plane, y] = (label == colour).astype(F32)
        return carry

    lax.fori_loop(0, EXT - 1, seeds, 0)
    for z in range(N):
        seed[z + LOW, EXT - 1] = (spread_row(row19_in[z : z + 1, :]) == colour).astype(F32)
    for y in range(N):
        seed[EXT - 1, y + LOW] = (spread_row(z_high[4, 4 * y + 7 : 4 * y + 8, :]) == colour).astype(F32)

    zero = jnp.zeros((8, X), F32)

    def apply(src, dst, low, high, products):
        rows = range(low + LOW, high + LOW + 1)

        def weight(plane, y, o):
            return spread_row(edge[plane, 4 * y + o : 4 * y + o + 1, :])

        start = low + LOW
        below = [weight(start - 1, y, 0) * (src[start - 1, y] - src[start, y]) for y in rows]

        def step(plane, carry):
            below, sums = carry
            above = []
            y0 = rows[0]
            here = src[plane, y0]
            flux_y_before = weight(plane, y0 - 1, 1) * (src[plane, y0 - 1] - here)
            plane_sums = [zero] * len(products)
            for y in rows:
                after = src[plane, y + 1]
                flux_z = weight(plane, y, 0) * (here - src[plane + 1, y])
                flux_y = weight(plane, y, 1) * (here - after)
                flux_x = weight(plane, y, 2) * (here - pltpu.roll(here, X - 1, 1))
                total = (flux_z - below[y - y0]) + (flux_y - flux_y_before) + (flux_x - pltpu.roll(flux_x, 1, 1))
                result = weight(plane, y, 3) * total
                dst[plane, y] = result
                if LOW <= y < LOW + N:
                    for i, f in enumerate(products):
                        plane_sums[i] = plane_sums[i] + f(here, result)
                above.append(flux_z)
                here = after
                flux_y_before = flux_y
            mine = jnp.logical_and(plane >= LOW, plane < LOW + N).astype(F32)
            sums = tuple(s + mine * t for s, t in zip(sums, plane_sums))
            return tuple(above), sums

        _, sums = lax.fori_loop(start, high + LOW + 1, step, (tuple(below), (zero,) * len(products)))
        return sums

    def square(here, result):
        return result * result

    def cross(here, result):
        return here * result

    (m0,) = apply(seed, w0, -2, 18, [square])
    m1, m2 = apply(w0, w1, -1, 17, [cross, square])
    m3, m4 = apply(w1, w2, 0, 16, [cross, square])

    def energy(plane, total):
        here = w2[plane, LOW]
        for y in range(LOW, LOW + N):
            after = w2[plane, y + 1]
            d_z = here - w2[plane + 1, y]
            d_y = here - after
            d_x = here - pltpu.roll(here, X - 1, 1)
            total = total + (
                spread_row(edge[plane, 4 * y : 4 * y + 1, :]) * (d_z * d_z)
                + spread_row(edge[plane, 4 * y + 1 : 4 * y + 2, :]) * (d_y * d_y)
                + spread_row(edge[plane, 4 * y + 2 : 4 * y + 3, :]) * (d_x * d_x)
            )
            here = after
        return total

    m5 = lax.fori_loop(LOW, LOW + N, energy, zero)

    packed = zero
    for j, m in enumerate((m0, m1, m2, m3, m4, m5)):
        packed = jnp.where(lane == 8 * j + sublane, jnp.sum(m, axis=1, keepdims=True), packed)
    row = jnp.sum(packed, axis=0, keepdims=True)

    def all_sum(row, slots, me, count, stage, device):
        part[stage] = row
        slots[pl.ds(me, 1)] = row[None]
        copies = []
        for i in range(1, count):
            copy = pltpu.make_async_remote_copy(
                src_ref=part.at[stage], dst_ref=slots.at[me], send_sem=psend_sem.at[stage, i - 1],
                recv_sem=precv_sem.at[stage, i - 1], device_id=device(lax.rem(me + i, count)), device_id_type=MESH,
            )
            copy.start()
            copies.append(copy)
        for copy in copies:
            copy.wait()
        return jnp.sum(slots[...], axis=0)

    row = all_sum(row, sum_z, gz, nz, 0, lambda i: (i, yx))
    row = all_sum(row, sum_y, yx, ny, 1, lambda i: (gz, i))

    row = spread_row(row)
    mu = [
        jnp.broadcast_to(jnp.sum(jnp.where(lane == 8 * j + sublane, row, 0.0), axis=1, keepdims=True), (8, X))
        for j in range(6)
    ]

    def form(a, b, shift):
        total = None
        for i, p in enumerate(a):
            for j, q in enumerate(b):
                m = mu[i + j] if shift is None else mu[i + j + 1] + shift * mu[i + j]
                total = p * q * m if total is None else total + p * q * m
        return total

    one = jnp.ones((8, X), F32)
    residual, direction, answer = [one], [one], [zero] * ITERS
    rr = mu[0]
    for iteration in range(ITERS):
        length = jnp.clip(rr / form(direction, direction, RIDGE), STEP_LOW, STEP_HIGH)
        for i, d in enumerate(direction):
            answer[i] = answer[i] + length * d
        if iteration + 1 == ITERS:
            break
        shifted = [zero] + direction
        applied = [RIDGE * d + s for d, s in zip(direction + [zero], shifted)]
        residual = [r - length * a for r, a in zip(residual + [zero], applied)]
        after = form(residual, residual, None)
        beta = jnp.clip(after / rr, 0.0, BETA_HIGH)
        direction = [r + beta * d for r, d in zip(residual, direction + [zero])]
        rr = after

    def finish(z, carry):
        for y in range(N):
            at = (z + LOW, y + LOW)
            value = seed[at] - (answer[0] * w0[at] + answer[1] * w1[at] + answer[2] * w2[at])
            prob_ref[pl.ds(z * N + y, FIELDS, stride=N * N), :] = value
        return carry

    lax.fori_loop(0, N, finish, 0)


def body(features, conv_weight, conv_bias, labels):
    taps = jnp.pad(conv_weight.transpose(3, 4, 0, 2, 1), ((0, 0), (0, 0), (0, 1), (0, 0), (0, 0)))
    taps = jnp.concatenate([taps, taps], axis=2).reshape(72, 3 * CH)
    vmem = pl.BlockSpec(memory_space=pltpu.VMEM)
    strips = [
        pltpu.VMEM((N + 2, 16, X), F32), pltpu.VMEM((N + 2, 16, X), F32),
        pltpu.VMEM((4, ROWS, X), F32), pltpu.VMEM((5, ROWS, X), F32),
        pltpu.VMEM((4, 16, X), F32), pltpu.VMEM((4, 16, X), F32),
        pltpu.VMEM((4, 16, X), F32), pltpu.VMEM((4, 16, X), F32),
        pltpu.VMEM((N, X), F32),
    ]
    prob, aff = pl.pallas_call(
        kernel,
        out_shape=(
            jax.ShapeDtypeStruct((FIELDS * N * N, X), F32),
            jax.ShapeDtypeStruct((3 * N * N, X), F32),
        ),
        in_specs=[pl.BlockSpec(memory_space=pl.ANY), vmem, pl.BlockSpec(memory_space=pltpu.SMEM), vmem],
        out_specs=(vmem, vmem),
        scratch_shapes=[
            pltpu.VMEM((N + 4, CH * N, X), jnp.bfloat16),
            pltpu.VMEM((240, 3 * CH * N), jnp.bfloat16),
            pltpu.VMEM((N + 2, N, X), F32),
            pltpu.VMEM((N + 2, ROWS, X), F32),
            pltpu.VMEM((N, X), F32),
            *strips,
            pltpu.VMEM((EXT, 96, X), F32),
            pltpu.VMEM((EXT, 96, X), F32),
            pltpu.VMEM((EXT, EXT, 8, X), F32),
            pltpu.VMEM((EXT, EXT, 8, X), F32),
            pltpu.VMEM((EXT, EXT, 8, X), F32),
            pltpu.VMEM((EXT, EXT, 8, X), F32),
            pltpu.VMEM((2, 1, X), F32),
            pltpu.VMEM((8, 1, X), F32),
            pltpu.VMEM((32, 1, X), F32),
            pltpu.SemaphoreType.DMA((CH,)),
            pltpu.SemaphoreType.DMA((9,)),
            pltpu.SemaphoreType.DMA((9,)),
            pltpu.SemaphoreType.DMA((2, 31)),
            pltpu.SemaphoreType.DMA((2, 31)),
        ],
        compiler_params=pltpu.CompilerParams(collective_id=0, has_side_effects=True, vmem_limit_bytes=40 * 2**20),
    )(features, taps, conv_bias, labels)
    return prob.reshape(FIELDS, N, N, X), aff.reshape(3, N, N, X)


def solution(mesh):
    in_specs = (P(None, "gz", "yx", None), P(), P(), P("gz", "yx", None))
    out_specs = (P(None, "gz", "yx", None), P(None, "gz", "yx", None))
    return jax.shard_map(body, mesh=mesh, in_specs=in_specs, out_specs=out_specs, check_vma=False)
```

time: 508 us -> 47.5 us (0.09)
  blocking collectives: 379 us -> 0 us
  starting transfers between devices: 62.5 us -> 0 us
  Pallas kernels: 0 us -> 42 us
  waiting for transfers between devices: 25.1 us -> 0 us
  other arithmetic: 19.6 us -> 0.04 us
  matrix products: 13.6 us -> 0 us
    psum x5 -> x0, blocking collectives: 379 us -> none  [the longest x3 227 us: squares(): return lax.psum(field_sums(residual, residual), ('gz', 'yx'))]
    ppermute x22 -> x0, starting transfers between devices: 62.5 us -> none  [the longest x10 37.1 us: padded_2(): lax.ppermute(tail, axis, [(i, (i + 1) % count) for i in range(ends)])]
    pallas_call x0 -> x1, Pallas kernels: none -> 42 us  [body(): pl.pallas_call(kernel, out_shape=(jax.ShapeDtypeStruct((FIELDS * N * N, X...]
    ppermute x22 -> x0, waiting for transfers between devices: 25.1 us -> none  [the longest x10 24.9 us: padded_2(): lax.ppermute(head, axis, [((i + 1) % count, i) for i in range(ends)])]
    dot_general x27 -> x0, matrix products: 13.6 us -> none  [conv_region(): jnp.einsum('oc,czyx->ozyx', conv_weight[:, :, offset_z, offset_y, offset_...]
    reduce_sum x5 -> x0, other arithmetic: 7.21 us -> none  [field_sums(): return jnp.sum(left * right, axis=(1, 2, 3))]
    convert_element_type x11 -> x0, other arithmetic: 5.13 us -> none  [the longest x4 3.34 us: operate(): field.astype(jnp.bfloat16)]
  transfers between devices with their start and end apart: 22 -> 0, of which waited for: 10 -> 0; matrix products, arithmetic and copies ran while one was open for 1% -> 0% of each run, Pallas kernels for 0% -> 0%
where the time goes in v1:
time: 47.5 us; the launch traced here: 47.3 us
  Pallas kernels  42 us (88%)
  local copies, waits for them, and re-layouts  4.59 us (10%)
  between operations  0.68 us (1%)
    pallas_call x1, Pallas kernels, body(): pl.pallas_call(kernel, out_shape=(jax.ShapeDtypeStruct((FIELDS * N * N, X...  42 us
    unnamed x8, local copies, waits for them, and re-layouts  3.69 us

profile of v1, /device:TPU:1, one launch (start us, length us, event | category | flops | bytes accessed | tf_op | source)
XLA Modules:
  0.0 47.3 jit_solution(1300655714971514676)
XLA Ops:
  0.6 0.8 %pad.4 = bf16[3,3,4,3,16]{4,1,0,3,2:T(4,128)(2,1)S(1)} pad(bf16[3,3,3,3,16]{4,1,0,3,2:T(4,128)(2,1)} %bitcast.5, bf16[]{:T(256)} %constant.2.clone.1), padding=0_0x0_0x0_1x0_0x0_0 | pad | bytes 6050 | tf_op jit(solution)/shard_map/jit(_pad)/pad | solution.py:380
  1.4 0.0 copy-start.1
  1.5 0.0 copy-start.2
  1.5 0.1 reshape.13.taps_ref
  1.6 0.7 %copy-done.1 = s32[16,16,128]{2,1,0:T(8,128)S(1)} copy-done((s32[16,16,128]{2,1,0:T(8,128)S(1)}, s32[16,16,128]{2,1,0:T(8,128)}, u32[]{:S(2)}) %copy-start.1) | copy-done | bytes 131096
  2.3 0.0 copy-done.2
  2.4 0.0 copy-start
  2.4 1.2 %copy-done = bf16[16,16,16,128]{3,2,1,0:T(8,128)(2,1)S(1)} copy-done((bf16[16,16,16,128]{3,2,1,0:T(8,128)(2,1)S(1)}, bf16[16,16,16,128]{3,2,1,0:T(8,128)(2,1)}, u32[]{:S(2)}) %copy-start) | copy-done | bytes 1048600
  3.6 42.0 %shard_map.59 = (f32[2048,128]{1,0:T(8,128)S(1)}, f32[768,128]{1,0:T(8,128)S(1)}) custom-call(bf16[16,16,16,128]{3,2,1,0:T(8,128)(2,1)S(1)} %copy-done, bf16[72,48]{1,0:T(8,128)(2,1)S(1)} %reshape.13.taps_ref, f32[3]{0:T(128)S(1)} %copy-done.2, s32[16,16,128]{2,1,0:T(8,128)S(1)} %copy-done.1), custom_call_target="tpu_custom_call" | custom-call | tf_op jit(solution)/shard_map/pallas_call | solution.py:390
  45.6 1.0 %copy.10 = f32[8,16,16,128]{3,2,1,0:T(8,128)} copy(f32[8,16,16,128]{3,2,1,0:T(8,128)S(1)} %bitcast.3) | data formatting | bytes 2097152
  46.6 0.7 %copy.11 = f32[3,16,16,128]{3,2,1,0:T(8,128)} copy(f32[3,16,16,128]{3,2,1,0:T(8,128)S(1)} %bitcast.4) | data formatting | bytes 786432
  (2 shorter events, 0.1 us)
Async XLA Ops:
  1.4 0.9 %copy-start.1 = (s32[16,16,128]{2,1,0:T(8,128)S(1)}, s32[16,16,128]{2,1,0:T(8,128)}, u32[]{:S(2)}) copy-start(s32[16,16,128]{2,1,0:T(8,128)} %labels_ref.1) | copy-start | bytes 393220
  1.5 0.9 %copy-start.2 = (f32[3]{0:T(128)S(1)}, f32[3]{0:T(128)}, u32[]{:S(2)}) copy-start(f32[3]{0:T(128)} %bias_ref.1) | copy-start | bytes 40
  2.4 1.2 %copy-start = (bf16[16,16,16,128]{3,2,1,0:T(8,128)(2,1)S(1)}, bf16[16,16,16,128]{3,2,1,0:T(8,128)(2,1)}, u32[]{:S(2)}) copy-start(bf16[16,16,16,128]{3,2,1,0:T(8,128)(2,1)} %feat_ref.1) | copy-start | bytes 3145732

commit v2 on v1

v2 whole, which is shorter than its diff:
```python
import jax
import jax.numpy as jnp
from jax import lax
from jax.experimental import pallas as pl
from jax.experimental.pallas import tpu as pltpu
from jax.sharding import PartitionSpec as P

FEATURE_ORDER = (*range(6), *range(10, 16), *range(6, 10))
MESH = pl.DeviceIdType.MESH
FIELDS = 8
ITERS = 3
RIDGE = 0.5
N = 16
X = 128
CH = 16
LOW = 3
EXT = N + 7
ROWS = 4 * (N + 2)
F32 = jnp.float32

STEP_LOW, STEP_HIGH = 1.0 / 12.5, 2.0
BETA_HIGH = 25.0


def lane_iota(shape):
    return lax.broadcasted_iota(jnp.int32, shape, len(shape) - 1)


def row_iota(shape):
    return lax.broadcasted_iota(jnp.int32, shape, len(shape) - 2)


def spread_row(row):
    return jnp.broadcast_to(row, (8, X))


def build_weights(conv_ref, rows_ref, taps_ref, lhs_ref):
    rows_ref[...] = jnp.zeros_like(rows_ref)
    for o in range(3):
        for dz in range(3):
            for dy in range(3):
                at = ((o * 3 + dz) * 3 + dy) * 3
                rows_ref[at : at + 3, 0:CH] = conv_ref[o, dz, dy].astype(F32)
    expand = (lax.div(lane_iota((X, CH * N)), N) == row_iota((X, CH * N))).astype(jnp.bfloat16)
    taps_ref[...] = jnp.dot(rows_ref[...].astype(jnp.bfloat16), expand, preferred_element_type=F32)
    columns = CH * N
    y_in = lax.rem(lane_iota((8, columns)), N)
    kind = lax.rem(row_iota((8, columns)), 4)
    half = lax.div(row_iota((8, columns)), 4)
    for dx in range(3):
        for dz in range(3):
            taps = []
            for dy in range(3):
                tap = jnp.zeros((8, columns), F32)
                for o in range(3):
                    at = ((o * 3 + dz) * 3 + dy) * 3 + dx
                    tap = jnp.where(kind == o, jnp.broadcast_to(taps_ref[at : at + 1, :], (8, columns)), tap)
                taps.append(tap)
            for pair in range(0, (N + 2) // 2, 2):
                blocks = []
                for p in (pair, pair + 1):
                    block = jnp.zeros((8, columns), F32)
                    if p < (N + 2) // 2:
                        gap = y_in - (2 * p - 1 + half) + 1
                        for dy in range(3):
                            block = jnp.where(gap == dy, taps[dy], block)
                    blocks.append(block)
                at = dx * 80 + pair * 8
                lhs_ref[at : at + 16, dz * columns : (dz + 1) * columns] = jnp.concatenate(blocks, axis=0).astype(jnp.bfloat16)


def sigmoid(x):
    e = jnp.exp(-jnp.abs(x))
    s = 1.0 / (1.0 + e)
    return jnp.where(x >= 0.0, s, e * s)


def kernel(
    feat_ref, conv_ref, bias_ref, labels_ref,
    basis_ref, answer_ref, aff_ref,
    conv, bias_v, feat, taps_rows, taps, lhs, labels, lab, own, row19,
    y_low, y_high, z_low, z_high, low_low, low_high, high_low, high_high, row19_in,
    raw, edge, mark, mark_left, mark_right, w0, w1, w2,
    part, sum_z, sum_y, aff_v, answer_v,
    feat_sem, label_sem, small_sem, out_sem, send_sem, recv_sem, psend_sem, precv_sem,
):
    gz, yx = lax.axis_index("gz"), lax.axis_index("yx")
    nz, ny = lax.axis_size("gz"), lax.axis_size("yx")
    z_up, z_dn = lax.rem(gz + 1, nz), lax.rem(gz + nz - 1, nz)
    y_up, y_dn = lax.rem(yx + 1, ny), lax.rem(yx + ny - 1, ny)

    barrier = pltpu.get_barrier_semaphore()
    count = 0
    for dz in (z_dn, gz, z_up):
        for dy in (y_dn, yx, y_up):
            if dz is gz and dy is yx:
                continue
            pl.semaphore_signal(barrier, inc=1, device_id=(dz, dy), device_id_type=MESH)
            count += 1
    for i in range(2, nz - 1):
        pl.semaphore_signal(barrier, inc=1, device_id=(lax.rem(gz + i, nz), yx), device_id_type=MESH)
        count += 1
    for i in range(2, ny - 1):
        pl.semaphore_signal(barrier, inc=1, device_id=(gz, lax.rem(yx + i, ny)), device_id_type=MESH)
        count += 1

    load_conv = pltpu.make_async_copy(conv_ref, conv, small_sem.at[0])
    load_bias = pltpu.make_async_copy(bias_ref, bias_v, small_sem.at[1])
    load_conv.start()
    load_bias.start()
    loads = [
        pltpu.make_async_copy(feat_ref.at[:, z], feat.at[z + 2], feat_sem.at[z])
        for z in range(N)
    ]
    load_labels = pltpu.make_async_copy(labels_ref, labels, label_sem)
    load_labels.start()
    for z in FEATURE_ORDER:
        loads[z].start()

    for p in (0, 1, N + 2, N + 3):
        feat[p] = jnp.zeros((CH, N, X), jnp.bfloat16)
    lab[0] = jnp.zeros((N, X), F32)
    lab[N + 1] = jnp.zeros((N, X), F32)
    load_conv.wait()
    load_bias.wait()
    build_weights(conv, taps_rows, taps, lhs)
    load_labels.wait()
    for z in range(N):
        lab[z + 1] = labels[z].astype(F32)
    for z in range(N):
        row19[z : z + 1, :] = lab[z + 1, 3:4, :]

    sublane = row_iota((8, X))
    lane = lane_iota((8, X))
    first, last = lane == 0, lane == X - 1
    zero = jnp.zeros((8, X), F32)

    def two_planes(j):
        plane = 2 * j
        left = feat[pl.ds(plane, 3)].reshape(3 * CH * N, X)
        right = feat[pl.ds(plane + 1, 3)].reshape(3 * CH * N, X)
        both = jnp.concatenate([left, right], axis=1)
        out = jnp.dot(lhs[...], both, preferred_element_type=F32)
        for h in range(2):
            for p in range((N + 2) // 2):
                at = 8 * p
                a = out[at : at + 8, h * X : (h + 1) * X]
                b = out[80 + at : 80 + at + 8, h * X : (h + 1) * X]
                c = out[160 + at : 160 + at + 8, h * X : (h + 1) * X]
                total = (
                    b
                    + jnp.where(first, 0.0, pltpu.roll(a, 1, 1))
                    + jnp.where(last, 0.0, pltpu.roll(c, X - 1, 1))
                )
                y = 2 * p - 1
                if y >= 0:
                    total = jnp.where(sublane == 3, spread_row(lab[plane + h, y : y + 1, :]), total)
                if y + 1 < N:
                    total = jnp.where(sublane == 7, spread_row(lab[plane + h, y + 1 : y + 2, :]), total)
                own[plane + h, at : at + 8, :] = total

    copies = []

    def send(src, dst, to):
        i = len(copies)
        copy = pltpu.make_async_remote_copy(
            src_ref=src, dst_ref=dst, send_sem=send_sem.at[i], recv_sem=recv_sem.at[i], device_id=to, device_id_type=MESH
        )
        copy.start()
        copies.append(copy)

    bottom, top = pl.ds(0, 16), pl.ds(ROWS - 16, 16)
    here = set()
    for chunk, pairs in enumerate(((0, 1, 2), (6, 7, 8), (3, 4, 5))):
        for z in FEATURE_ORDER:
            if z not in here and 2 * pairs[0] - 2 <= z <= 2 * pairs[-1] + 1:
                loads[z].wait()
                here.add(z)
        for j in pairs:
            two_planes(j)
        if chunk == 0:
            pl.semaphore_wait(barrier, count)
            send(row19, row19_in, (gz, y_dn))
        six = pl.ds(2 * pairs[0], 6)
        send(own.at[six, top, :], y_low.at[six], (gz, y_up))
        send(own.at[six, bottom, :], y_high.at[six], (gz, y_dn))
        if chunk == 0:
            send(own.at[pl.ds(0, 5)], z_high, (z_dn, yx))
            send(own.at[pl.ds(0, 4), top, :], high_low, (z_dn, y_up))
            send(own.at[pl.ds(0, 4), bottom, :], high_high, (z_dn, y_dn))
        if chunk == 1:
            send(own.at[pl.ds(N - 2, 4)], z_low, (z_up, yx))
            send(own.at[pl.ds(N - 2, 4), top, :], low_low, (z_up, y_up))
            send(own.at[pl.ds(N - 2, 4), bottom, :], low_high, (z_up, y_dn))

    has_zl, has_zh = (gz > 0).astype(F32), (gz < nz - 1).astype(F32)
    has_yl, has_yh = (yx > 0).astype(F32), (yx < ny - 1).astype(F32)
    kind = lax.rem(sublane, 4)
    bias = zero
    for o in range(3):
        bias = jnp.where(kind == o, jnp.broadcast_to(bias_v[0:1, o : o + 1], (8, X)), bias)
    keep_x = jnp.where((kind == 2) & last, 0.0, 1.0)
    is_label = kind == 3

    def plane_weights(plane, own_plane, zn, zn_plane, has_z, corner_low, corner_high, yn_plane, rows=range(11)):
        z = plane - LOW
        global_z = gz * N + z
        inside = jnp.logical_and(global_z >= 0, global_z < nz * N - 1).astype(F32)
        keep_zx = jnp.where(kind == 0, inside, keep_x)
        for v in rows:
            terms = []
            if 1 <= v <= 9:
                if own_plane is not None:
                    terms.append(own[own_plane, 8 * (v - 1) : 8 * v, :])
                if zn is not None:
                    terms.append(has_z * zn[zn_plane, 8 * (v - 1) : 8 * v, :])
            if v <= 1:
                if yn_plane is not None:
                    terms.append(has_yl * y_low[yn_plane, 8 * v : 8 * v + 8, :])
                if corner_low is not None:
                    terms.append((has_yl * has_z) * corner_low[zn_plane, 8 * v : 8 * v + 8, :])
            if v >= 9:
                if yn_plane is not None:
                    terms.append(has_yh * y_high[yn_plane, 8 * (v - 9) : 8 * (v - 9) + 8, :])
                if corner_high is not None:
                    terms.append((has_yh * has_z) * corner_high[zn_plane, 8 * (v - 9) : 8 * (v - 9) + 8, :])
            total = terms[0]
            for term in terms[1:]:
                total = total + term
            a = sigmoid(total + bias)
            raw[plane, 8 * v : 8 * v + 8, :] = jnp.where(is_label, (total == 0.0).astype(F32), a)
            mark[plane, 8 * v : 8 * v + 8, :] = total
            mark_right[plane, 8 * v : 8 * v + 8, :] = pltpu.roll(total, X - 1, 1)
            keep = keep_zx
            if v == 1:
                keep = jnp.where(sublane == 1, has_yl, keep)
            if v == 9:
                keep = jnp.where(sublane == 1, has_yh, keep)
            kept = a * keep
            before = pltpu.roll(jnp.where(is_label, total, kept), 1, 1)
            mark_left[plane, 8 * v : 8 * v + 8, :] = before
            edge[plane, 8 * v : 8 * v + 8, :] = jnp.where(is_label, pltpu.roll(before, 1, 0), kept)

    def middle(rows, carry):
        def step(z, carry):
            plane_weights(z + LOW, z + 1, None, None, None, None, None, z + 1, rows)
            return carry

        lax.fori_loop(1, N - 1, step, carry)

    middle(range(2, 9), 0)
    for copy in copies:
        copy.wait()
    middle((0, 1, 9, 10), 0)
    for z in (-3, -2):
        plane_weights(z + LOW, None, z_low, z + 3, has_zl, low_low, low_high, None)
    for z in (-1, 0):
        plane_weights(z + LOW, z + 1, z_low, z + 3, has_zl, low_low, low_high, z + 1)
    for z in (15, 16):
        plane_weights(z + LOW, z + 1, z_high, z - 15, has_zh, high_low, high_high, z + 1)
    for z in (17, 18):
        plane_weights(z + LOW, None, z_high, z - 15, has_zh, high_low, high_high, None)

    def affinities_out(z, carry):
        for o in range(3):
            for h in range(2):
                at = pl.multiple_of(o * N * N + z * N + 8 * h, 8)
                aff_v[pl.ds(at, 8), :] = raw[z + LOW, pl.ds(4 * LOW + 32 * h + o, 8, stride=4), :]
        return carry

    lax.fori_loop(0, N, affinities_out, 0)
    stores = [pltpu.make_async_copy(aff_v, aff_ref, out_sem.at[0])]
    stores[-1].start()

    for z in range(N):
        mark[z + LOW, 4 * (EXT - 1) + 3 : 4 * EXT, :] = row19_in[z : z + 1, :]
    mark[EXT - 1, 8 : 8 + ROWS, :] = z_high[4]

    colour = (sublane + 1).astype(F32)

    def weight(plane, y, o):
        return spread_row(edge[plane, 4 * y + o : 4 * y + o + 1, :])

    def unseeded(plane, y):
        return spread_row(raw[plane, 4 * y + 3 : 4 * y + 4, :])

    def planes(body, low, high, group, carry):
        start, count = low + LOW, high - low + 1

        def step(i, carry):
            for g in range(group):
                carry = body(start + i * group + g, carry)
            return carry

        carry = lax.fori_loop(0, count // group, step, carry)
        for plane in range(start + count // group * group, start + count):
            carry = body(plane, carry)
        return carry

    def in_block(plane):
        return jnp.logical_and(plane >= LOW, plane < LOW + N).astype(F32)

    def first_step(plane, m0):
        plane_sum = zero
        before_w = weight(plane, 0, 1)
        for y in range(LOW - 2, LOW + N + 3):
            at = 4 * y + 3
            after_w = weight(plane, y, 1)
            total = zero
            for marks, where, w in (
                (mark, (plane - 1, at), weight(plane - 1, y, 0)),
                (mark, (plane + 1, at), weight(plane, y, 0)),
                (mark, (plane, at - 4), before_w),
                (mark, (plane, at + 4), after_w),
                (mark_left, (plane, at), weight(plane, y, 3)),
                (mark_right, (plane, at), weight(plane, y, 2)),
            ):
                label = spread_row(marks[where[0], where[1] : where[1] + 1, :])
                total = total - jnp.where(label == colour, w, 0.0)
            result = unseeded(plane, y) * total
            w0[plane, y] = result
            if LOW <= y < LOW + N:
                plane_sum = plane_sum + result * result
            before_w = after_w
        return m0 + in_block(plane) * plane_sum

    def store_block(i, w):
        inner = pl.ds(LOW, N)
        copy = pltpu.make_async_copy(w.at[inner, inner], basis_ref.at[i], out_sem.at[i + 1])
        copy.start()
        stores.append(copy)

    m0 = planes(first_step, -2, 18, 3, zero)
    store_block(0, w0)

    def apply(src, dst, low, high, group):
        rows = range(low + LOW, high + LOW + 1)
        y0 = rows[0]

        def step(plane, carry):
            below, crosses, squares = carry
            above = []
            here = src[plane, y0]
            flux_y_before = weight(plane, y0 - 1, 1) * (src[plane, y0 - 1] - here)
            cross = square = zero
            for y in rows:
                after = src[plane, y + 1]
                flux_z = weight(plane, y, 0) * (here - src[plane + 1, y])
                flux_y = weight(plane, y, 1) * (here - after)
                right = weight(plane, y, 2) * (here - pltpu.roll(here, X - 1, 1))
                left = weight(plane, y, 3) * (here - pltpu.roll(here, 1, 1))
                total = ((flux_z - below[y - y0]) + (flux_y - flux_y_before)) + (right + left)
                result = unseeded(plane, y) * total
                dst[plane, y] = result
                if LOW <= y < LOW + N:
                    cross = cross + here * result
                    square = square + result * result
                above.append(flux_z)
                here = after
                flux_y_before = flux_y
            mine = in_block(plane)
            return tuple(above), crosses + mine * cross, squares + mine * square

        start = low + LOW
        below = tuple(weight(start - 1, y, 0) * (src[start - 1, y] - src[start, y]) for y in rows)
        return planes(step, low, high, group, (below, zero, zero))[1:]

    m1, m2 = apply(w0, w1, -1, 17, 3)
    store_block(1, w1)
    m3, m4 = apply(w1, w2, 0, 16, 3)
    store_block(2, w2)

    def energy(plane, total):
        here = w2[plane, LOW]
        sums = zero
        for y in range(LOW, LOW + N):
            after = w2[plane, y + 1]
            d_z = here - w2[plane + 1, y]
            d_y = here - after
            d_x = here - pltpu.roll(here, X - 1, 1)
            sums = sums + (
                weight(plane, y, 0) * (d_z * d_z) + weight(plane, y, 1) * (d_y * d_y) + weight(plane, y, 2) * (d_x * d_x)
            )
            here = after
        return total + sums

    m5 = planes(energy, 0, N - 1, 4, zero)

    packed = zero
    for j, m in enumerate((m0, m1, m2, m3, m4, m5)):
        packed = jnp.where(lane == 8 * j + sublane, jnp.sum(m, axis=1, keepdims=True), packed)
    row = jnp.sum(packed, axis=0, keepdims=True)

    def all_sum(row, slots, me, count, stage, device):
        part[stage] = row
        slots[pl.ds(me, 1)] = row[None]
        copies = []
        for i in range(1, count):
            copy = pltpu.make_async_remote_copy(
                src_ref=part.at[stage], dst_ref=slots.at[me], send_sem=psend_sem.at[stage, i - 1],
                recv_sem=precv_sem.at[stage, i - 1], device_id=device(lax.rem(me + i, count)), device_id_type=MESH,
            )
            copy.start()
            copies.append(copy)
        for copy in copies:
            copy.wait()
        return jnp.sum(slots[...], axis=0)

    row = all_sum(row, sum_z, gz, nz, 0, lambda i: (i, yx))
    row = all_sum(row, sum_y, yx, ny, 1, lambda i: (gz, i))

    row = spread_row(row)
    mu = [
        jnp.broadcast_to(jnp.sum(jnp.where(lane == 8 * j + sublane, row, 0.0), axis=1, keepdims=True), (8, X))
        for j in range(6)
    ]

    def form(a, b, shift):
        total = None
        for i, p in enumerate(a):
            for j, q in enumerate(b):
                m = mu[i + j] if shift is None else mu[i + j + 1] + shift * mu[i + j]
                total = p * q * m if total is None else total + p * q * m
        return total

    one = jnp.ones((8, X), F32)
    residual, direction, answer = [one], [one], [zero] * ITERS
    rr = mu[0]
    for iteration in range(ITERS):
        length = jnp.clip(rr / form(direction, direction, RIDGE), STEP_LOW, STEP_HIGH)
        for i, d in enumerate(direction):
            answer[i] = answer[i] + length * d
        if iteration + 1 == ITERS:
            break
        shifted = [zero] + direction
        applied = [RIDGE * d + s for d, s in zip(direction + [zero], shifted)]
        residual = [r - length * a for r, a in zip(residual + [zero], applied)]
        after = form(residual, residual, None)
        beta = jnp.clip(after / rr, 0.0, BETA_HIGH)
        direction = [r + beta * d for r, d in zip(residual, direction + [zero])]
        rr = after

    for i in range(ITERS):
        answer_v[i] = answer[i]
    copy = pltpu.make_async_copy(answer_v, answer_ref, out_sem.at[4])
    copy.start()
    stores.append(copy)
    for copy in stores:
        copy.wait()


CHUNKS = 2
DEEP = N // CHUNKS


def finish_kernel(basis_ref, answer_ref, labels_ref, aff_in_ref, prob_ref, aff_ref, basis, answer, labels, prob, aff_v, in_sem, small_sem, out_sem):
    affinities = pltpu.make_async_copy(aff_in_ref, aff_v, small_sem.at[2])
    small = [
        pltpu.make_async_copy(answer_ref, answer, small_sem.at[0]),
        pltpu.make_async_copy(labels_ref, labels, small_sem.at[1]),
    ]
    for copy in small:
        copy.start()
    loads = []
    for j in range(CHUNKS):
        part = pl.ds(j * DEEP, DEEP)
        load = pltpu.make_async_copy(basis_ref.at[:, part], basis.at[:, part], in_sem.at[j])
        load.start()
        loads.append(load)
    affinities.start()
    for copy in small:
        copy.wait()
    colour = row_iota((8, X)) + 1
    a, b, c = (answer[i] for i in range(ITERS))
    stores = []
    for j in range(CHUNKS):
        loads[j].wait()

        def plane(z, carry):
            for y in range(N):
                seed = jnp.where(spread_row(labels[z, y : y + 1, :]) == colour, 1.0, 0.0)
                value = seed - (a * basis[0, z, y] + b * basis[1, z, y] + c * basis[2, z, y])
                prob[pl.ds(z * N + y, FIELDS, stride=N * N), :] = value
            return carry

        lax.fori_loop(j * DEEP, (j + 1) * DEEP, plane, 0)
        part = pl.ds(j * DEEP * N, DEEP * N)
        copy = pltpu.make_async_copy(prob.reshape(FIELDS, N * N, X).at[:, part], prob_ref.at[:, part], out_sem.at[j])
        copy.start()
        stores.append(copy)
        if j == 0:
            affinities.wait()
            affinities = pltpu.make_async_copy(aff_v, aff_ref, small_sem.at[2])
            affinities.start()
    stores.append(affinities)
    for copy in stores:
        copy.wait()


def body(features, conv_weight, conv_bias, labels):
    taps = conv_weight.transpose(0, 2, 3, 4, 1)
    vmem = pl.BlockSpec(memory_space=pltpu.VMEM)
    hbm = pl.BlockSpec(memory_space=pltpu.HBM)
    strips = [
        pltpu.VMEM((N + 2, 16, X), F32), pltpu.VMEM((N + 2, 16, X), F32),
        pltpu.VMEM((4, ROWS, X), F32), pltpu.VMEM((5, ROWS, X), F32),
        pltpu.VMEM((4, 16, X), F32), pltpu.VMEM((4, 16, X), F32),
        pltpu.VMEM((4, 16, X), F32), pltpu.VMEM((4, 16, X), F32),
        pltpu.VMEM((N, X), F32),
    ]
    basis, answer, aff = pl.pallas_call(
        kernel,
        out_shape=(
            jax.ShapeDtypeStruct((ITERS, N, N, FIELDS, X), F32),
            jax.ShapeDtypeStruct((ITERS, FIELDS, X), F32),
            jax.ShapeDtypeStruct((3 * N * N, X), F32),
        ),
        in_specs=[hbm] * 4,
        out_specs=(hbm,) * 3,
        scratch_shapes=[
            pltpu.VMEM((3, 3, 3, 3, CH), jnp.bfloat16),
            pltpu.VMEM((1, 3), F32),
            pltpu.VMEM((N + 4, CH, N, X), jnp.bfloat16),
            pltpu.VMEM((96, X), F32),
            pltpu.VMEM((96, CH * N), F32),
            pltpu.VMEM((240, 3 * CH * N), jnp.bfloat16),
            pltpu.VMEM((N, N, X), jnp.int32),
            pltpu.VMEM((N + 2, N, X), F32),
            pltpu.VMEM((N + 2, ROWS, X), F32),
            pltpu.VMEM((N, X), F32),
            *strips,
            pltpu.VMEM((EXT, 96, X), F32),
            pltpu.VMEM((EXT, 96, X), F32),
            pltpu.VMEM((EXT, 96, X), F32),
            pltpu.VMEM((EXT, 96, X), F32),
            pltpu.VMEM((EXT, 96, X), F32),
            pltpu.VMEM((EXT, EXT, 8, X), F32),
            pltpu.VMEM((EXT, EXT, 8, X), F32),
            pltpu.VMEM((EXT, EXT, 8, X), F32),
            pltpu.VMEM((2, 1, X), F32),
            pltpu.VMEM((8, 1, X), F32),
            pltpu.VMEM((32, 1, X), F32),
            pltpu.VMEM((3 * N * N, X), F32),
            pltpu.VMEM((ITERS, FIELDS, X), F32),
            pltpu.SemaphoreType.DMA((N,)),
            pltpu.SemaphoreType.DMA,
            pltpu.SemaphoreType.DMA((2,)),
            pltpu.SemaphoreType.DMA((5,)),
            pltpu.SemaphoreType.DMA((13,)),
            pltpu.SemaphoreType.DMA((13,)),
            pltpu.SemaphoreType.DMA((2, 31)),
            pltpu.SemaphoreType.DMA((2, 31)),
        ],
        compiler_params=pltpu.CompilerParams(collective_id=0, has_side_effects=True, vmem_limit_bytes=60 * 2**20),
    )(features, taps, conv_bias[None], labels)
    prob, aff = pl.pallas_call(
        finish_kernel,
        out_shape=(jax.ShapeDtypeStruct((FIELDS, N * N, X), F32), jax.ShapeDtypeStruct((3 * N * N, X), F32)),
        in_specs=[hbm] * 4,
        out_specs=(hbm, hbm),
        scratch_shapes=[
            pltpu.VMEM((ITERS, N, N, FIELDS, X), F32),
            pltpu.VMEM((ITERS, FIELDS, X), F32),
            pltpu.VMEM((N, N, X), jnp.int32),
            pltpu.VMEM((FIELDS * N * N, X), F32),
            pltpu.VMEM((3 * N * N, X), F32),
            pltpu.SemaphoreType.DMA((CHUNKS,)),
            pltpu.SemaphoreType.DMA((3,)),
            pltpu.SemaphoreType.DMA((CHUNKS,)),
        ],
        compiler_params=pltpu.CompilerParams(vmem_limit_bytes=60 * 2**20),
    )(basis, answer, labels, aff)
    return prob.reshape(FIELDS, N, N, X), aff.reshape(3, N, N, X)


def solution(mesh):
    in_specs = (P(None, "gz", "yx", None), P(), P(), P("gz", "yx", None))
    out_specs = (P(None, "gz", "yx", None), P(None, "gz", "yx", None))
    return jax.shard_map(body, mesh=mesh, in_specs=in_specs, out_specs=out_specs, check_vma=False)
```

time: 47.5 us -> 39.9 us (0.84)
  local copies, waits for them, and re-layouts: 4.59 us -> 0 us
  Pallas kernels: 42 us -> 39.1 us
    unnamed x8 -> x0, local copies, waits for them, and re-layouts: 3.69 us -> none
    pallas_call x1 -> x2, Pallas kernels: 42 us -> 39.1 us  [the longest x1 35.8 us: body(): pl.pallas_call(kernel, out_shape=(jax.ShapeDtypeStruct((ITERS, N, N, FIEL...]
    pad x1 -> x0, local copies, waits for them, and re-layouts: 0.77 us -> none  [body(): jnp.pad(conv_weight.transpose(3, 4, 0, 2, 1), ((0, 0), (0, 0), (0, 1), (0...]
where the time goes in v2:
time: 39.9 us; the launch traced here: 39.7 us
  Pallas kernels  39.1 us (98%)
  between operations  0.64 us (2%)
    pallas_call x1, Pallas kernels, body(): pl.pallas_call(kernel, out_shape=(jax.ShapeDtypeStruct((ITERS, N, N, FIEL...  35.8 us
    pallas_call x1, Pallas kernels, body(): pl.pallas_call(finish_kernel, out_shape=(jax.ShapeDtypeStruct((FIELDS, N...  3.28 us

profile of v2, /device:TPU:1, one launch (start us, length us, event | category | flops | bytes accessed | tf_op | source)
XLA Modules:
  0.0 39.7 jit_solution(1877563703965409427)
XLA Ops:
  0.6 35.8 %shard_map.59 = (f32[3,16,16,8,128]{4,3,2,1,0:T(8,128)}, f32[3,8,128]{2,1,0:T(8,128)}, f32[768,128]{1,0:T(8,128)}) custom-call(bf16[16,16,16,128]{3,2,1,0:T(8,128)(2,1)} %feat_ref.1, bf16[3,3,3,3,16]{4,3,2,1,0:T(4,128)(2,1)} %bitcast.4, f32[1,3]{1,0:T(1,128)} %bitcast.5, s32[16,16,128]{2,1,0:T(8,128)} %labels_ref.3), custom_call_target="tpu_custom_call" | custom-call | tf_op jit(solution)/shard_map/pallas_call | solution.py:511
  36.5 3.3 %shard_map.60 = (f32[8,256,128]{2,1,0:T(8,128)}, f32[768,128]{1,0:T(8,128)}) custom-call(f32[3,16,16,8,128]{4,3,2,1,0:T(8,128)} %get-tuple-element.7.basis_ref, f32[3,8,128]{2,1,0:T(8,128)} %get-tuple-element.8.answer_ref, s32[16,16,128]{2,1,0:T(8,128)} %labels_ref.3, f32[768,128]{1,0:T(8,128)} %get-tuple-element.9.aff_in_ref), custom_call_target="tpu_custom_call" | custom-call | tf_op jit(solution)/shard_map/pallas_call | solution.py:556

commit v3 on v2

--- a/solution.py
+++ b/solution.py
@@ -241,17 +241,19 @@
             mark_left[plane, 8 * v : 8 * v + 8, :] = before
             edge[plane, 8 * v : 8 * v + 8, :] = jnp.where(is_label, pltpu.roll(before, 1, 0), kept)
 
-    def middle(rows, carry):
-        def step(z, carry):
-            plane_weights(z + LOW, z + 1, None, None, None, None, None, z + 1, rows)
+    def middle(rows, group):
+        def step(i, carry):
+            for g in range(group):
+                z = 1 + i * group + g
+                plane_weights(z + LOW, z + 1, None, None, None, None, None, z + 1, rows)
             return carry
 
-        lax.fori_loop(1, N - 1, step, carry)
-
-    middle(range(2, 9), 0)
+        lax.fori_loop(0, (N - 2) // group, step, 0)
+
+    middle(range(2, 9), 14)
     for copy in copies:
         copy.wait()
-    middle((0, 1, 9, 10), 0)
+    middle((0, 1, 9, 10), 14)
     for z in (-3, -2):
         plane_weights(z + LOW, None, z_low, z + 3, has_zl, low_low, low_high, None)
     for z in (-1, 0):
@@ -330,7 +332,7 @@
         copy.start()
         stores.append(copy)
 
-    m0 = planes(first_step, -2, 18, 3, zero)
+    m0 = planes(first_step, -2, 18, 7, zero)
     store_block(0, w0)
 
     def apply(src, dst, low, high, group):
@@ -365,9 +367,9 @@
         below = tuple(weight(start - 1, y, 0) * (src[start - 1, y] - src[start, y]) for y in rows)
         return planes(step, low, high, group, (below, zero, zero))[1:]
 
-    m1, m2 = apply(w0, w1, -1, 17, 3)
+    m1, m2 = apply(w0, w1, -1, 17, 19)
     store_block(1, w1)
-    m3, m4 = apply(w1, w2, 0, 16, 3)
+    m3, m4 = apply(w1, w2, 0, 16, 17)
     store_block(2, w2)
 
     def energy(plane, total):
@@ -384,7 +386,7 @@
             here = after
         return total + sums
 
-    m5 = planes(energy, 0, N - 1, 4, zero)
+    m5 = planes(energy, 0, N - 1, 8, zero)
 
     packed = zero
     for j, m in enumerate((m0, m1, m2, m3, m4, m5)):

time: 39.9 us -> 37.7 us (0.945)
  Pallas kernels: 39.1 us -> 36.9 us
    pallas_call x1, Pallas kernels: 35.8 us -> 33.6 us  [body(): pl.pallas_call(kernel, out_shape=(jax.ShapeDtypeStruct((ITERS, N, N, FIEL...]
where the time goes in v3:
time: 37.7 us; the launch traced here: 37.5 us
  Pallas kernels  36.9 us (98%)
  between operations  0.64 us (2%)
    pallas_call x1, Pallas kernels, body(): pl.pallas_call(kernel, out_shape=(jax.ShapeDtypeStruct((ITERS, N, N, FIEL...  33.6 us
    pallas_call x1, Pallas kernels, body(): pl.pallas_call(finish_kernel, out_shape=(jax.ShapeDtypeStruct((FIELDS, N...  3.28 us

profile of v3, /device:TPU:1, one launch (start us, length us, event | category | flops | bytes accessed | tf_op | source)
XLA Modules:
  0.0 37.5 jit_solution(15268726394875078554)
XLA Ops:
  0.6 33.6 %shard_map.59 = (f32[3,16,16,8,128]{4,3,2,1,0:T(8,128)}, f32[3,8,128]{2,1,0:T(8,128)}, f32[768,128]{1,0:T(8,128)}) custom-call(bf16[16,16,16,128]{3,2,1,0:T(8,128)(2,1)} %feat_ref.1, bf16[3,3,3,3,16]{4,3,2,1,0:T(4,128)(2,1)} %bitcast.4, f32[1,3]{1,0:T(1,128)} %bitcast.5, s32[16,16,128]{2,1,0:T(8,128)} %labels_ref.3), custom_call_target="tpu_custom_call" | custom-call | tf_op jit(solution)/shard_map/pallas_call | solution.py:513
  34.3 3.3 %shard_map.60 = (f32[8,256,128]{2,1,0:T(8,128)}, f32[768,128]{1,0:T(8,128)}) custom-call(f32[3,16,16,8,128]{4,3,2,1,0:T(8,128)} %get-tuple-element.7.basis_ref, f32[3,8,128]{2,1,0:T(8,128)} %get-tuple-element.8.answer_ref, s32[16,16,128]{2,1,0:T(8,128)} %labels_ref.3, f32[768,128]{1,0:T(8,128)} %get-tuple-element.9.aff_in_ref), custom_call_target="tpu_custom_call" | custom-call | tf_op jit(solution)/shard_map/pallas_call | solution.py:558

commit v4 on v3

--- a/solution.py
+++ b/solution.py
@@ -168,7 +168,9 @@
         )
         copy.start()
         copies.append(copy)
-
+        return copy
+
+    row_copies = []
     bottom, top = pl.ds(0, 16), pl.ds(ROWS - 16, 16)
     here = set()
     for chunk, pairs in enumerate(((0, 1, 2), (6, 7, 8), (3, 4, 5))):
@@ -180,10 +182,10 @@
             two_planes(j)
         if chunk == 0:
             pl.semaphore_wait(barrier, count)
-            send(row19, row19_in, (gz, y_dn))
+            row_copies.append(send(row19, row19_in, (gz, y_dn)))
         six = pl.ds(2 * pairs[0], 6)
-        send(own.at[six, top, :], y_low.at[six], (gz, y_up))
-        send(own.at[six, bottom, :], y_high.at[six], (gz, y_dn))
+        row_copies.append(send(own.at[six, top, :], y_low.at[six], (gz, y_up)))
+        row_copies.append(send(own.at[six, bottom, :], y_high.at[six], (gz, y_dn)))
         if chunk == 0:
             send(own.at[pl.ds(0, 5)], z_high, (z_dn, yx))
             send(own.at[pl.ds(0, 4), top, :], high_low, (z_dn, y_up))
@@ -250,10 +252,66 @@
 
         lax.fori_loop(0, (N - 2) // group, step, 0)
 
+    colour = (sublane + 1).astype(F32)
+
+    def weight(plane, y, o):
+        return spread_row(edge[plane, 4 * y + o : 4 * y + o + 1, :])
+
+    def unseeded(plane, y):
+        return spread_row(raw[plane, 4 * y + 3 : 4 * y + 4, :])
+
+    def planes(body, low, high, group, carry):
+        start, count = low + LOW, high - low + 1
+
+        def step(i, carry):
+            for g in range(group):
+                carry = body(start + i * group + g, carry)
+            return carry
+
+        carry = lax.fori_loop(0, count // group, step, carry)
+        for plane in range(start + count // group * group, start + count):
+            carry = body(plane, carry)
+        return carry
+
+    def in_block(plane):
+        return jnp.logical_and(plane >= LOW, plane < LOW + N).astype(F32)
+
+    def first_step(*runs):
+        def step(plane, m0):
+            plane_sum = zero
+            for low, high in runs:
+                before_w = weight(plane, low + LOW - 1, 1)
+                for y in range(low + LOW, high + LOW + 1):
+                    at = 4 * y + 3
+                    after_w = weight(plane, y, 1)
+                    total = zero
+                    for marks, where, w in (
+                        (mark, (plane - 1, at), weight(plane - 1, y, 0)),
+                        (mark, (plane + 1, at), weight(plane, y, 0)),
+                        (mark, (plane, at - 4), before_w),
+                        (mark, (plane, at + 4), after_w),
+                        (mark_left, (plane, at), weight(plane, y, 3)),
+                        (mark_right, (plane, at), weight(plane, y, 2)),
+                    ):
+                        label = spread_row(marks[where[0], where[1] : where[1] + 1, :])
+                        total = total - jnp.where(label == colour, w, 0.0)
+                    result = unseeded(plane, y) * total
+                    w0[plane, y] = result
+                    if LOW <= y < LOW + N:
+                        plane_sum = plane_sum + result * result
+                    before_w = after_w
+            return m0 + in_block(plane) * plane_sum
+
+        return step
+
     middle(range(2, 9), 14)
-    for copy in copies:
+    m0 = planes(first_step((2, 13)), 2, 13, 6, zero)
+    for copy in row_copies:
         copy.wait()
     middle((0, 1, 9, 10), 14)
+    for copy in copies:
+        if all(copy is not done for done in row_copies):
+            copy.wait()
     for z in (-3, -2):
         plane_weights(z + LOW, None, z_low, z + 3, has_zl, low_low, low_high, None)
     for z in (-1, 0):
@@ -270,61 +328,11 @@
                 aff_v[pl.ds(at, 8), :] = raw[z + LOW, pl.ds(4 * LOW + 32 * h + o, 8, stride=4), :]
         return carry
 
-    lax.fori_loop(0, N, affinities_out, 0)
     stores = [pltpu.make_async_copy(aff_v, aff_ref, out_sem.at[0])]
-    stores[-1].start()
 
     for z in range(N):
         mark[z + LOW, 4 * (EXT - 1) + 3 : 4 * EXT, :] = row19_in[z : z + 1, :]
     mark[EXT - 1, 8 : 8 + ROWS, :] = z_high[4]
-
-    colour = (sublane + 1).astype(F32)
-
-    def weight(plane, y, o):
-        return spread_row(edge[plane, 4 * y + o : 4 * y + o + 1, :])
-
-    def unseeded(plane, y):
-        return spread_row(raw[plane, 4 * y + 3 : 4 * y + 4, :])
-
-    def planes(body, low, high, group, carry):
-        start, count = low + LOW, high - low + 1
-
-        def step(i, carry):
-            for g in range(group):
-                carry = body(start + i * group + g, carry)
-            return carry
-
-        carry = lax.fori_loop(0, count // group, step, carry)
-        for plane in range(start + count // group * group, start + count):
-            carry = body(plane, carry)
-        return carry
-
-    def in_block(plane):
-        return jnp.logical_and(plane >= LOW, plane < LOW + N).astype(F32)
-
-    def first_step(plane, m0):
-        plane_sum = zero
-        before_w = weight(plane, 0, 1)
-        for y in range(LOW - 2, LOW + N + 3):
-            at = 4 * y + 3
-            after_w = weight(plane, y, 1)
-            total = zero
-            for marks, where, w in (
-                (mark, (plane - 1, at), weight(plane - 1, y, 0)),
-                (mark, (plane + 1, at), weight(plane, y, 0)),
-                (mark, (plane, at - 4), before_w),
-                (mark, (plane, at + 4), after_w),
-                (mark_left, (plane, at), weight(plane, y, 3)),
-                (mark_right, (plane, at), weight(plane, y, 2)),
-            ):
-                label = spread_row(marks[where[0], where[1] : where[1] + 1, :])
-                total = total - jnp.where(label == colour, w, 0.0)
-            result = unseeded(plane, y) * total
-            w0[plane, y] = result
-            if LOW <= y < LOW + N:
-                plane_sum = plane_sum + result * result
-            before_w = after_w
-        return m0 + in_block(plane) * plane_sum
 
     def store_block(i, w):
         inner = pl.ds(LOW, N)
@@ -332,7 +340,9 @@
         copy.start()
         stores.append(copy)
 
-    m0 = planes(first_step, -2, 18, 7, zero)
+    m0 = planes(first_step((-2, 1), (14, 18)), 2, 13, 12, m0)
+    m0 = planes(first_step((-2, 18)), -2, 1, 4, m0)
+    m0 = planes(first_step((-2, 18)), 14, 18, 5, m0)
     store_block(0, w0)
 
     def apply(src, dst, low, high, group):
@@ -393,23 +403,26 @@
         packed = jnp.where(lane == 8 * j + sublane, jnp.sum(m, axis=1, keepdims=True), packed)
     row = jnp.sum(packed, axis=0, keepdims=True)
 
-    def all_sum(row, slots, me, count, stage, device):
+    def all_sum(row, slots, me, count, stage, device, hops):
         part[stage] = row
         slots[pl.ds(me, 1)] = row[None]
         copies = []
-        for i in range(1, count):
+        for i in sorted(range(1, count), key=hops, reverse=True):
             copy = pltpu.make_async_remote_copy(
                 src_ref=part.at[stage], dst_ref=slots.at[me], send_sem=psend_sem.at[stage, i - 1],
                 recv_sem=precv_sem.at[stage, i - 1], device_id=device(lax.rem(me + i, count)), device_id_type=MESH,
             )
             copy.start()
             copies.append(copy)
+        if stage == 0:
+            lax.fori_loop(0, N, affinities_out, 0)
+            stores[0].start()
         for copy in copies:
             copy.wait()
         return jnp.sum(slots[...], axis=0)
 
-    row = all_sum(row, sum_z, gz, nz, 0, lambda i: (i, yx))
-    row = all_sum(row, sum_y, yx, ny, 1, lambda i: (gz, i))
+    row = all_sum(row, sum_z, gz, nz, 0, lambda i: (i, yx), lambda i: min(i, nz - i))
+    row = all_sum(row, sum_y, yx, ny, 1, lambda i: (gz, i), lambda i: min(i % 8, 8 - i % 8) + min(i // 8, 4 - i // 8))
 
     row = spread_row(row)
     mu = [

time: 37.7 us -> 37.4 us (level)
  no operation moved by 1% of the time
where the time goes in v4:
time: 37.4 us; the launch traced here: 37.3 us
  Pallas kernels  36.6 us (98%)
  between operations  0.64 us (2%)
    pallas_call x1, Pallas kernels, body(): pl.pallas_call(kernel, out_shape=(jax.ShapeDtypeStruct((ITERS, N, N, FIEL...  33.3 us
    pallas_call x1, Pallas kernels, body(): pl.pallas_call(finish_kernel, out_shape=(jax.ShapeDtypeStruct((FIELDS, N...  3.28 us

profile of v4, /device:TPU:1, one launch (start us, length us, event | category | flops | bytes accessed | tf_op | source)
XLA Modules:
  0.0 37.3 jit_solution(8161262954773308816)
XLA Ops:
  0.6 33.3 %shard_map.59 = (f32[3,16,16,8,128]{4,3,2,1,0:T(8,128)}, f32[3,8,128]{2,1,0:T(8,128)}, f32[768,128]{1,0:T(8,128)}) custom-call(bf16[16,16,16,128]{3,2,1,0:T(8,128)(2,1)} %feat_ref.1, bf16[3,3,3,3,16]{4,3,2,1,0:T(4,128)(2,1)} %bitcast.4, f32[1,3]{1,0:T(1,128)} %bitcast.5, s32[16,16,128]{2,1,0:T(8,128)} %labels_ref.3), custom_call_target="tpu_custom_call" | custom-call | tf_op jit(solution)/shard_map/pallas_call | solution.py:526
  34.0 3.3 %shard_map.60 = (f32[8,256,128]{2,1,0:T(8,128)}, f32[768,128]{1,0:T(8,128)}) custom-call(f32[3,16,16,8,128]{4,3,2,1,0:T(8,128)} %get-tuple-element.7.basis_ref, f32[3,8,128]{2,1,0:T(8,128)} %get-tuple-element.8.answer_ref, s32[16,16,128]{2,1,0:T(8,128)} %labels_ref.3, f32[768,128]{1,0:T(8,128)} %get-tuple-element.9.aff_in_ref), custom_call_target="tpu_custom_call" | custom-call | tf_op jit(solution)/shard_map/pallas_call | solution.py:571
